TPU v7x, 32 devices: a whole 2x2x4 slice. The times are simulated.
32 devices in a mesh: member: 8 (over z, core), fsdp: 4 (over y, x).
Axes of the slice: x: 2, y: 2, z: 4, core: 2. Of those that a mesh axis runs over, the one named last changes fastest.
Arguments:
- attn_queries: bfloat16 [8, 512, 16, 128], P('member', 'fsdp'), may hold values from -27 to 27
- attn_keys: bfloat16 [8, 512, 16, 128], P('member', 'fsdp'), may hold values from -7.5 to 7.5
- attn_values: bfloat16 [8, 512, 16, 128], P('member', 'fsdp'), may hold values from -6 to 6
- out_grad: bfloat16 [8, 512, 4096], P('member', 'fsdp'), may hold values from -6 to 6
- out_proj: bfloat16 [8, 4096, 2048], P('member', 'fsdp'), may hold values from -0.125 to 0.125
- first_moment: float32 [8, 4096, 2048], P('member', 'fsdp'), may hold values from -4 to 4
- second_moment: float32 [8, 4096, 2048], P('member', 'fsdp'), may hold values from 0.05 to 5
- explore_noise: bfloat16 [8, 4096, 2048], P('member', 'fsdp'), may hold values from -0.4375 to 0.4375
- donor_index: int32 [8], replicated, may hold values from 0 to 7, as said below
- copy_flag: int32 [8], replicated, may hold values from 0 to 1, as said below
Outputs:
- new_proj: bfloat16 [8, 4096, 2048], P('member', 'fsdp')
- new_first: float32 [8, 4096, 2048], P('member', 'fsdp')
- new_second: float32 [8, 4096, 2048], P('member', 'fsdp')
Inputs may be any that keep to these rules, and one draw needn't show every extreme that they name: `donor_index`: every entry names one of the same four members (which four may differ from call to call); none of those four has copy_flag 1. `copy_flag`: exactly 2 entries are 1.
All inputs are finite; a program needn't handle non-finite values.
Results may differ from a plain program's by a relative error of at most 0.017.
Values may be sent and summed in bfloat16 or wider, within the bound.
A program may use at most 128 MiB of HBM per device.

v0:
```python
import jax
import jax.numpy as jnp
from jax import lax
from jax.sharding import PartitionSpec as P

masked_value = -1e30
beta_first = 0.9
beta_second = 0.95
learn_rate = 0.001
decay_rate = 0.1
epsilon = 1e-08


def shortened(array):
    return jax.tree.map(lambda a: a.astype(jnp.bfloat16) if a.dtype == jnp.float32 else a, array)


def group_attention(items):
    queries, keys, values = items
    sequence, single, head_count, head_size = queries.shape
    queries = queries.reshape(sequence, head_count, head_size)
    keys = keys.reshape(sequence, head_count, head_size)
    values = values.reshape(sequence, head_count, head_size)
    scores = jnp.einsum(
        "qhe,khe->hqk", queries, keys, preferred_element_type=jnp.float32
    ) * head_size ** (-0.5)
    position = lax.iota(jnp.int32, sequence)
    allowed = position[:, None] >= position[None, :]
    scores = jnp.where(allowed[None], scores, masked_value)
    maximum = jnp.max(scores, axis=-1, keepdims=True)
    weights = jnp.where(allowed[None], jnp.exp(scores - maximum), jnp.float32(0.0))
    totals = jnp.sum(weights, axis=-1)
    context = jnp.einsum(
        "hqk,khe->qhe", weights.astype(jnp.bfloat16), values, preferred_element_type=jnp.float32
    )
    context = context / jnp.transpose(totals)[:, :, None]
    return context.astype(jnp.bfloat16).reshape(sequence, single, head_count, head_size)


def body(
    attn_queries,
    attn_keys,
    attn_values,
    out_grad,
    out_proj,
    first_moment,
    second_moment,
    explore_noise,
    donor_index,
    copy_flag,
):
    group_count = lax.axis_size("fsdp")
    token_count, head_count, head_size = attn_queries.shape[1:]
    width = head_count * head_size
    grouped = (head_count // group_count, head_size)
    query_groups = attn_queries[0].reshape(token_count, group_count, grouped[0], grouped[1])
    key_groups = attn_keys[0].reshape(token_count, group_count, grouped[0], grouped[1])
    value_groups = attn_values[0].reshape(token_count, group_count, grouped[0], grouped[1])
    context_groups = group_attention(
        (
            lax.all_to_all(query_groups, "fsdp", split_axis=1, concat_axis=0, tiled=True),
            lax.all_to_all(key_groups, "fsdp", split_axis=1, concat_axis=0, tiled=True),
            lax.all_to_all(value_groups, "fsdp", split_axis=1, concat_axis=0, tiled=True),
        )
    )
    context = lax.all_to_all(
        context_groups, "fsdp", split_axis=0, concat_axis=1, tiled=True
    ).reshape(token_count, width)
    grad_tokens = out_grad[0]
    row_count = out_proj.shape[1]
    columns = lax.all_to_all(grad_tokens, "fsdp", split_axis=1, concat_axis=0, tiled=True)
    running = jnp.zeros((row_count, width), jnp.float32)
    shard_piece = lax.all_gather(context, "fsdp", axis=0, tiled=True)
    for number in range(shard_piece.shape[0] // token_count):
        context_rows = shard_piece[number * token_count : (number + 1) * token_count]
        grad_rows = lax.dynamic_slice_in_dim(columns, number * token_count, token_count, 0)
        partial_sum = lax.dot_general(
            grad_rows, context_rows, (((0,), (0,)), ((), ())), preferred_element_type=jnp.float32
        )
        running = running + lax.optimization_barrier(partial_sum.astype(jnp.bfloat16)).astype(
            jnp.float32
        )
    moment_one = beta_first * first_moment[0] + (1.0 - beta_first) * running
    moment_two = beta_second * second_moment[0] + (1.0 - beta_second) * running * running
    bias_first = 1.0 - beta_first**100.0
    bias_second = 1.0 - beta_second**100.0
    step_size = moment_one / bias_first / (jnp.sqrt(moment_two / bias_second) + epsilon)
    weight_float = out_proj[0].astype(jnp.float32)
    updated = (weight_float - learn_rate * (step_size + decay_rate * weight_float)).astype(
        jnp.bfloat16
    )
    member_count = lax.axis_size("member")
    slice_rows = row_count // member_count
    source = jnp.where(copy_flag == 1, donor_index, lax.iota(jnp.int32, member_count))
    spread_weight = updated.reshape(member_count, slice_rows, width)
    spread_first = moment_one.reshape(member_count, slice_rows, width)
    spread_second = moment_two.reshape(member_count, slice_rows, width)
    chosen_weight = jnp.take(
        lax.all_to_all(spread_weight, "member", split_axis=0, concat_axis=0, tiled=True),
        source,
        axis=0,
    )
    taken_weight = lax.all_to_all(chosen_weight, "member", split_axis=0, concat_axis=0, tiled=True)
    first_slices = lax.all_to_all(
        spread_first.astype(jnp.bfloat16), "member", split_axis=0, concat_axis=0, tiled=True
    ).astype(spread_first.dtype)
    second_slices = lax.all_to_all(
        spread_second.astype(jnp.bfloat16), "member", split_axis=0, concat_axis=0, tiled=True
    ).astype(spread_second.dtype)
    chosen_first = jnp.take(first_slices, source, axis=0)
    chosen_second = jnp.take(second_slices, source, axis=0)
    taken_first = lax.all_to_all(
        shortened(chosen_first), "member", split_axis=0, concat_axis=0, tiled=True
    ).astype(chosen_first.dtype)
    taken_second = lax.all_to_all(
        shortened(chosen_second), "member", split_axis=0, concat_axis=0, tiled=True
    ).astype(chosen_second.dtype)
    taken_weight = taken_weight.reshape(row_count, width)
    own_member = lax.axis_index("member")
    flagged = copy_flag[own_member] == 1
    perturbed = (taken_weight.astype(jnp.float32) + explore_noise[0].astype(jnp.float32)).astype(
        jnp.bfloat16
    )
    new_proj = jnp.where(flagged, perturbed, taken_weight)
    new_first = taken_first.reshape(row_count, width)
    new_second = taken_second.reshape(row_count, width)
    return (new_proj[None], new_first[None], new_second[None])


def solution(mesh):
    return jax.shard_map(
        body,
        mesh=mesh,
        in_specs=(
            P("member", "fsdp", None, None),
            P("member", "fsdp", None, None),
            P("member", "fsdp", None, None),
            P("member", "fsdp", None),
            P("member", "fsdp", None),
            P("member", "fsdp", None),
            P("member", "fsdp", None),
            P("member", "fsdp", None),
            P(),
            P(),
        ),
        out_specs=(P("member", "fsdp", None), P("member", "fsdp", None), P("member", "fsdp", None)),
        check_vma=False,
    )
```

profile of v0, /device:TPU:0, one launch (start us, length us, event | category | flops | bytes accessed | tf_op | source)
XLA Modules:
  0.0 757.7 jit_solution(16620804242662702706)
XLA Ops:
  7.2 2.0 copy.73
  9.2 5.2 all-to-all-start.1
  14.4 2.0 copy.71
  16.3 6.0 all-to-all-done.1
  22.4 3.5 all-to-all-start
  25.9 0.9 copy.75
  26.8 6.2 all-to-all-done
  33.0 3.5 all-to-all-start.2
  36.5 0.1 iota_compare_fusion
  36.7 6.3 all-to-all-done.2
  43.1 3.4 fusion.34
  46.5 2.6 fusion.21
  49.1 0.4 copy.78
  49.5 9.7 %all_to_all.106 = bf16[512,1,4,128]{3,2,1,0:T(4,128)(2,1)S(1)} all-to-all(bf16[512,1,4,128]{3,2,1,0:T(4,128)(2,1)S(1)} %copy.78), channel_id=1, replica_groups=mesh['member'=8,'fsdp'=4] {'fsdp'}, dimensions={0} | all-to-all | bytes 1048576 | tf_op jit(solution)/shard_map/all_to_all | solution.py:66
  59.2 0.1 copy.79
  59.3 1.0 copy.80
  60.3 1.3 copy.81
  61.6 3.7 all-to-all-start.4
  65.3 9.4 %copy.70 = f32[1,1024,2048]{1,2,0:T(8,128)} copy(f32[1,1024,2048]{2,1,0:T(8,128)} %param.17) | data formatting | bytes 16777216 | tf_op args[5]
  74.7 9.2 %copy.86 = f32[1,1024,2048]{1,2,0:T(8,128)} copy(f32[1,1024,2048]{2,1,0:T(8,128)} %param.18) | data formatting | bytes 16777216 | tf_op args[6]
  83.9 6.4 copy.69
  90.4 9.4 %all-gather.2.cloned.1.call-done = bf16[512,2048]{0,1:T(8,128)(2,1)} async-done(((bf16[128,2048]{0,1:T(8,128)(2,1)}), bf16[512,2048]{0,1:T(8,128)(2,1)}) %all-gather.2.cloned.1.call-update) | async-done | bytes 2097168 | tf_op jit(solution)/shard_map/all_gather | solution.py:73
  99.8 4.5 convert_bitcast_fusion.3
  104.2 3.4 convert_bitcast_fusion.2
  107.6 3.2 convert_bitcast_fusion.1
  110.9 3.3 convert_bitcast_fusion
  114.2 16.7 %fusion.33 = (bf16[1024,2048]{0,1:T(8,128)(2,1)}, bf16[1024,2048]{0,1:T(8,128)(2,1)}, bf16[1024,2048]{0,1:T(8,128)(2,1)}) fusion(bf16[1024,2048]{0,1:T(8,128)(2,1)} %convert_bitcast_fusion, bf16[1024,2048]{0,1:T(8,128)(2,1)} %convert_bitcast_fusion.1, bf16[1024,2048]{0,1:T(8,128)(2,1)} %convert_bitcast_fusion.2, ...), kind=kLoop, calls=%fused_computation.53 | loop fusion | flops 54525952 | bytes 50331648 | tf_op jit(solution)/shard_map/convert_element_type | solution.py:108
  130.9 6.6 copy.91
  137.5 4.6 all-to-all-start.5
  142.1 6.5 copy.92
  148.6 87.6 %all-to-all-done.5 = bf16[8,128,2048]{2,1,0:T(8,128)(2,1)} async-done(((bf16[8,128,2048]{2,1,0:T(8,128)(2,1)}), bf16[8,128,2048]{2,1,0:T(8,128)(2,1)}, u32[]{:S(2)}, u32[]{:S(2)}) %all-to-all-start.5) | async-done | bytes 4194336 | tf_op jit(solution)/shard_map/all_to_all | solution.py:99
  236.2 4.6 all-to-all-start.7
  240.8 6.4 copy.93
  247.2 87.6 %all-to-all-done.7 = bf16[8,128,2048]{2,1,0:T(8,128)(2,1)} async-done(((bf16[8,128,2048]{2,1,0:T(8,128)(2,1)}), bf16[8,128,2048]{2,1,0:T(8,128)(2,1)}, u32[]{:S(2)}, u32[]{:S(2)}) %all-to-all-start.7) | async-done | bytes 4194336 | tf_op jit(solution)/shard_map/all_to_all | solution.py:104
  334.8 5.0 all-to-all-start.9
  339.8 4.9 gather_fusion
  344.8 5.0 gather_fusion.1
  349.8 83.8 %all-to-all-done.9 = bf16[8,128,2048]{2,1,0:T(8,128)(2,1)} async-done(((bf16[8,128,2048]{2,1,0:T(8,128)(2,1)}), bf16[8,128,2048]{2,1,0:T(8,128)(2,1)}, u32[]{:S(2)}, u32[]{:S(2)}) %all-to-all-start.9) | async-done | bytes 4194336 | tf_op jit(solution)/shard_map/all_to_all | solution.py:107
  433.6 5.0 gather_fusion.2
  438.6 9.0 %select_convert_fusion = (bf16[8,128,2048]{2,1,0:T(8,128)(2,1)S(1)}, bf16[8,128,2048]{2,1,0:T(8,128)(2,1)S(1)}, bf16[8,128,2048]{2,1,0:T(8,128)(2,1)}) fusion(bf16[8,128,2048]{2,1,0:T(8,128)(2,1)} %gather_fusion.2, pred[8]{0:T(512)(128)(4,1)S(1)} %get-tuple-element.4, bf16[8,128,2048]{2,1,0:T(8,128)(2,1)} %gather_fusion.1, bf16[8,128,2048]{2,1,0:T(8,128)(2,1)} %gather_fusion), kind=kLoop, calls=%fused_computation.12 | loop fusion | flops 6291456 | bytes 25165832 | tf_op jit(solution)/shard_map/convert_element_type | solution.py:15
  447.5 97.3 %all_to_all.107 = bf16[8,128,2048]{2,1,0:T(8,128)(2,1)} all-to-all(bf16[8,128,2048]{2,1,0:T(8,128)(2,1)S(1)} %get-tuple-element.9), channel_id=1, replica_groups=mesh['member'=8,'fsdp'=4] {'member'}, dimensions={0} | all-to-all | bytes 8388608 | tf_op jit(solution)/shard_map/all_to_all | solution.py:115
  544.9 97.3 %all_to_all.108 = bf16[8,128,2048]{2,1,0:T(8,128)(2,1)} all-to-all(bf16[8,128,2048]{2,1,0:T(8,128)(2,1)S(1)} %get-tuple-element.10), channel_id=1, replica_groups=mesh['member'=8,'fsdp'=4] {'member'}, dimensions={0} | all-to-all | bytes 8388608 | tf_op jit(solution)/shard_map/all_to_all | solution.py:112
  642.2 4.6 all-to-all-start.6
  646.8 0.6 dynamic_slice.23
  648.0 6.8 bitcast_convert_fusion
  654.8 4.4 bitcast_convert_fusion.1
  659.3 81.5 %all-to-all-done.6 = bf16[8,128,2048]{2,1,0:T(8,128)(2,1)} async-done(((bf16[8,128,2048]{2,1,0:T(8,128)(2,1)}), bf16[8,128,2048]{2,1,0:T(8,128)(2,1)}, u32[]{:S(2)}, u32[]{:S(2)}) %all-to-all-start.6) | async-done | bytes 4194336 | tf_op jit(solution)/shard_map/all_to_all | solution.py:103
  740.8 10.1 %fusion.5 = bf16[1,1024,2048]{2,1,0:T(8,128)(2,1)} fusion(bf16[1,1024,2048]{2,1,0:T(8,128)(2,1)} %param.19, pred[]{:T(512)} %bitcast, bf16[1,1024,2048]{2,1,0:T(8,128)(2,1)} %bitcast.89), kind=kLoop, calls=%fused_computation.16 | loop fusion | flops 10485760 | bytes 12582913 | tf_op jit(solution)/shard_map/jit(_where)/select_n | solution.py:124
  (27 shorter events, 0.2 us)
Async XLA Ops:
  7.2 18.7 %copy-start.4 = (bf16[1,128,16,128]{3,2,1,0:T(8,128)(2,1)S(1)}, bf16[1,128,16,128]{3,2,1,0:T(8,128)(2,1)}, u32[]{:S(2)}) copy-start(bf16[1,128,16,128]{3,2,1,0:T(8,128)(2,1)} %param.14) | copy-start | bytes 1572868
  9.2 13.2 %all-to-all-start.1 = ((bf16[128,4,4,128]{3,0,2,1:T(8,128)(2,1)}), bf16[128,4,4,128]{3,0,2,1:T(8,128)(2,1)S(1)}, u32[]{:S(2)}, u32[]{:S(2)}) async-start(bf16[128,4,4,128]{3,0,2,1:T(8,128)(2,1)} %bitcast.7), calls=%async_computation.1 | async-start | bytes 1048576 | tf_op jit(solution)/shard_map/all_to_all | solution.py:62
  22.4 10.6 %all-to-all-start = ((bf16[128,4,4,128]{3,0,2,1:T(8,128)(2,1)}), bf16[128,4,4,128]{3,0,2,1:T(8,128)(2,1)S(1)}, u32[]{:S(2)}, u32[]{:S(2)}) async-start(bf16[128,4,4,128]{3,0,2,1:T(8,128)(2,1)} %bitcast.3), calls=%async_computation | async-start | bytes 1048576 | tf_op jit(solution)/shard_map/all_to_all | solution.py:61
  33.0 10.0 %all-to-all-start.2 = ((bf16[128,4,4,128]{3,0,2,1:T(8,128)(2,1)}), bf16[128,4,4,128]{3,0,2,1:T(8,128)(2,1)S(1)}, u32[]{:S(2)}, u32[]{:S(2)}) async-start(bf16[128,4,4,128]{3,0,2,1:T(8,128)(2,1)} %bitcast.11), calls=%async_computation.2 | async-start | bytes 1048576 | tf_op jit(solution)/shard_map/all_to_all | solution.py:63
  36.5 63.3 %all-gather.2.cloned.1.call-start = ((), (), s32[]{:S(2)}) async-start(), calls=%async_computation.11 | async-start | bytes 2621440 | tf_op jit(solution)/shard_map/all_gather | solution.py:73
  46.5 13.8 %copy-start.3 = (bf16[1,128,4096]{2,1,0:T(8,128)(2,1)S(1)}, bf16[1,128,4096]{2,1,0:T(8,128)(2,1)}, u32[]{:S(2)}) copy-start(bf16[1,128,4096]{2,1,0:T(8,128)(2,1)} %param.15) | copy-start | bytes 3145732
  61.6 28.7 %all-to-all-start.4 = ((bf16[128,4,1024]{0,2,1:T(8,128)(2,1)}), bf16[128,4,1024]{0,2,1:T(8,128)(2,1)S(1)}, u32[]{:S(2)}, u32[]{:S(2)}) async-start(bf16[128,4,1024]{0,2,1:T(8,128)(2,1)} %bitcast.21), calls=%async_computation.4 | async-start | bytes 2097152 | tf_op jit(solution)/shard_map/all_to_all | solution.py:71
  99.8 4.5 copy-start.2
  99.8 14.4 %slice-start = ((s8[8388608]{0:T(1024)(128)(4,1)}), s8[4194304]{0:T(1024)(128)(4,1)S(1)}, s32[]{:S(2)}) async-start(s8[8388608]{0:T(1024)(128)(4,1)} %bitcast.92), calls=%async_computation.12 | async-start | bytes 8388608
  104.2 9.9 %copy-start = (f32[1,1024,2048]{1,2,0:T(8,128)S(1)}, f32[1,1024,2048]{1,2,0:T(8,128)}, u32[]{:S(2)}) copy-start(f32[1,1024,2048]{1,2,0:T(8,128)} %copy.86) | copy-start | bytes 25165828
  107.6 6.5 slice-start.1
  137.5 98.7 %all-to-all-start.5 = ((bf16[8,128,2048]{2,1,0:T(8,128)(2,1)}), bf16[8,128,2048]{2,1,0:T(8,128)(2,1)}, u32[]{:S(2)}, u32[]{:S(2)}) async-start(bf16[8,128,2048]{2,1,0:T(8,128)(2,1)} %bitcast.98), calls=%async_computation.5 | async-start | bytes 8388608 | tf_op jit(solution)/shard_map/all_to_all | solution.py:99
  236.2 98.6 %all-to-all-start.7 = ((bf16[8,128,2048]{2,1,0:T(8,128)(2,1)}), bf16[8,128,2048]{2,1,0:T(8,128)(2,1)}, u32[]{:S(2)}, u32[]{:S(2)}) async-start(bf16[8,128,2048]{2,1,0:T(8,128)(2,1)} %bitcast.97), calls=%async_computation.7 | async-start | bytes 8388608 | tf_op jit(solution)/shard_map/all_to_all | solution.py:104
  334.8 5.0 copy-start.5
  334.8 5.0 copy-start.6
  334.8 98.8 %all-to-all-start.9 = ((bf16[8,128,2048]{2,1,0:T(8,128)(2,1)}), bf16[8,128,2048]{2,1,0:T(8,128)(2,1)}, u32[]{:S(2)}, u32[]{:S(2)}) async-start(bf16[8,128,2048]{2,1,0:T(8,128)(2,1)} %bitcast.96), calls=%async_computation.9 | async-start | bytes 8388608 | tf_op jit(solution)/shard_map/all_to_all | solution.py:107
  642.2 98.6 %all-to-all-start.6 = ((bf16[8,128,2048]{2,1,0:T(8,128)(2,1)}), bf16[8,128,2048]{2,1,0:T(8,128)(2,1)}, u32[]{:S(2)}, u32[]{:S(2)}) async-start(bf16[8,128,2048]{2,1,0:T(8,128)(2,1)} %get-tuple-element.11), calls=%async_computation.6 | async-start | bytes 8388608 | tf_op jit(solution)/shard_map/all_to_all | solution.py:103
  648.0 6.8 copy-start.1
Sparse Core Ops, SparseCore 0:
  60.4 39.2 all-gather.1
where the time goes:
time: 759 us; the launch traced here: 758 us
  waiting for transfers between devices  368 us (48%)
  blocking collectives  204 us (27%)
  local copies, waits for them, and re-layouts  68 us (9%)
  other arithmetic  47.1 us (6%)
  starting transfers between devices  34.6 us (5%)
  matrix products  20.4 us (3%)
  between operations  14.9 us (2%)
    all_to_all x1, blocking collectives, body(): lax.all_to_all(shortened(chosen_second), 'member', split_axis=0, concat_a...  97.3 us
    all_to_all x1, blocking collectives, body(): lax.all_to_all(shortened(chosen_first), 'member', split_axis=0, concat_ax...  97.3 us
    all_to_all x1, waiting for transfers between devices, body(): lax.all_to_all(spread_weight, 'member', split_axis=0, concat_axis=0, tile...  87.6 us
    all_to_all x1, waiting for transfers between devices, body(): lax.all_to_all(spread_first.astype(jnp.bfloat16), 'member', split_axis=0,...  87.6 us
    all_to_all x1, waiting for transfers between devices, body(): lax.all_to_all(spread_second.astype(jnp.bfloat16), 'member', split_axis=0...  83.8 us
    all_to_all x1, waiting for transfers between devices, body(): lax.all_to_all(chosen_weight, 'member', split_axis=0, concat_axis=0, tile...  81.5 us
    unnamed x25, local copies, waits for them, and re-layouts  31.3 us
    convert_element_type x1, other arithmetic, body(): spread_second.astype(jnp.bfloat16)  16.7 us
  transfers between devices with their start and end apart: 9, of which 8 were waited for; matrix products, arithmetic and copies ran while one was open for 8% of the time, Pallas kernels for 0%

commit v1 on v0

v1 whole, which is shorter than its diff:
```python
import functools

import jax
import jax.numpy as jnp
from jax import lax
from jax.experimental import pallas as pl
from jax.experimental.pallas import tpu as pltpu
from jax.sharding import PartitionSpec as P

masked_value = -1e30
beta_first = 0.9
beta_second = 0.95
learn_rate = 0.001
decay_rate = 0.1
epsilon = 1e-08
chunk_rows = 32
lag = 2
MESH = pl.DeviceIdType.MESH


def chain_kernel(size, chunks, flags, own_hbm, out_hbm, own, up, down, up_send, up_recv, down_send, down_recv, local_sem):
    me = lax.axis_index("member")
    last = size - 1
    load = pltpu.make_async_copy(own_hbm, own, local_sem)
    load.start()
    barrier = pltpu.get_barrier_semaphore()

    @pl.when(me > 0)
    def _():
        pl.semaphore_signal(barrier, inc=1, device_id={"member": me - 1}, device_id_type=MESH)

    @pl.when(me < last)
    def _():
        pl.semaphore_signal(barrier, inc=1, device_id={"member": me + 1}, device_id_type=MESH)

    @pl.when(jnp.logical_or(me == 0, me == last))
    def _():
        pl.semaphore_wait(barrier, 1)

    @pl.when(jnp.logical_and(me > 0, me < last))
    def _():
        pl.semaphore_wait(barrier, 2)

    load.wait()

    def rows(chunk):
        return pl.ds(pl.multiple_of(chunk * chunk_rows, chunk_rows), chunk_rows)

    def copy(buffer, send, recv, chunk, target):
        return pltpu.make_async_remote_copy(
            src_ref=buffer.at[rows(chunk)],
            dst_ref=buffer.at[rows(chunk)],
            send_sem=send.at[chunk],
            recv_sem=recv.at[chunk],
            device_id={"member": target},
            device_id_type=MESH,
        )

    def advance(chunk, buffer, send, recv, first, final, target, flag):
        @pl.when(jnp.logical_and(chunk >= 0, chunk < chunks))
        def _():
            @pl.when(first)
            def _():
                buffer[rows(chunk), :] = own[rows(chunk), :]

            @pl.when(jnp.logical_not(first))
            def _():
                copy(buffer, send, recv, chunk, target).wait_recv()
                buffer[rows(chunk), :] = lax.select(flag == 1, own[rows(chunk), :], buffer[rows(chunk), :])

            @pl.when(jnp.logical_not(final))
            def _():
                copy(buffer, send, recv, chunk, target).start()

    above = lax.rem(me + 1, size)
    below = lax.rem(me + size - 1, size)

    @pl.loop(0, chunks + lag * last)
    def _(step):
        advance(step - lag * me, up, up_send, up_recv, me == 0, me == last, above, flags[0])
        advance(step - lag * (last - me), down, down_send, down_recv, me == last, me == 0, below, flags[1])

    @pl.loop(0, chunks)
    def _(chunk):
        @pl.when(me < last)
        def _():
            copy(up, up_send, up_recv, chunk, above).wait_send()

        @pl.when(me > 0)
        def _():
            copy(down, down_send, down_recv, chunk, below).wait_send()

        part = lax.select(flags[2] == 1, up[rows(chunk), :], own[rows(chunk), :])
        own[rows(chunk), :] = lax.select(flags[3] == 1, down[rows(chunk), :], part)

    store = pltpu.make_async_copy(own, out_hbm, local_sem)
    store.start()
    store.wait()


def chain(flags, payload, size):
    chunks = payload.shape[0] // chunk_rows
    return pl.pallas_call(
        functools.partial(chain_kernel, size, chunks),
        out_shape=jax.ShapeDtypeStruct(payload.shape, payload.dtype),
        in_specs=[pl.BlockSpec(memory_space=pltpu.SMEM), pl.BlockSpec(memory_space=pl.ANY)],
        out_specs=pl.BlockSpec(memory_space=pl.ANY),
        scratch_shapes=[pltpu.VMEM(payload.shape, payload.dtype) for _ in range(3)]
        + [pltpu.SemaphoreType.DMA((chunks,)) for _ in range(4)]
        + [pltpu.SemaphoreType.DMA],
        compiler_params=pltpu.CompilerParams(
            collective_id=0, has_side_effects=True, vmem_limit_bytes=48 * 2**20
        ),
    )(flags, payload)


def group_attention(queries, keys, values):
    sequence, head_count, head_size = queries.shape
    scores = jnp.einsum(
        "qhe,khe->hqk", queries, keys, preferred_element_type=jnp.float32
    ) * head_size ** (-0.5)
    position = lax.iota(jnp.int32, sequence)
    allowed = position[:, None] >= position[None, :]
    scores = jnp.where(allowed[None], scores, masked_value)
    maximum = jnp.max(scores, axis=-1, keepdims=True)
    weights = jnp.where(allowed[None], jnp.exp(scores - maximum), jnp.float32(0.0))
    totals = jnp.sum(weights, axis=-1)
    context = jnp.einsum(
        "hqk,khe->qhe", weights.astype(jnp.bfloat16), values, preferred_element_type=jnp.float32
    )
    context = context / jnp.transpose(totals)[:, :, None]
    return context.astype(jnp.bfloat16).reshape(sequence, head_count * head_size)


def body(
    attn_queries,
    attn_keys,
    attn_values,
    out_grad,
    out_proj,
    first_moment,
    second_moment,
    explore_noise,
    donor_index,
    copy_flag,
):
    group_count = lax.axis_size("fsdp")
    member_count = lax.axis_size("member")
    token_count, head_count, head_size = attn_queries.shape[1:]
    width = head_count * head_size
    row_count = out_proj.shape[1]
    group_heads = head_count // group_count
    stacked = jnp.stack(
        [
            a[0].reshape(token_count, group_count, group_heads * head_size)
            for a in (attn_queries, attn_keys, attn_values)
        ]
    )
    stacked = jnp.transpose(stacked, (2, 0, 1, 3))
    columns = jnp.transpose(out_grad[0].reshape(token_count, group_count, row_count), (1, 0, 2))
    stacked = lax.all_to_all(stacked, "fsdp", split_axis=0, concat_axis=0, tiled=True)
    columns = lax.all_to_all(columns, "fsdp", split_axis=0, concat_axis=0, tiled=True)
    columns = columns.reshape(group_count * token_count, row_count)
    heads = jnp.transpose(stacked, (1, 0, 2, 3)).reshape(
        3, group_count * token_count, group_heads, head_size
    )
    context = group_attention(heads[0], heads[1], heads[2])
    context = lax.all_gather(context, "fsdp", axis=0)
    context = jnp.transpose(context, (1, 0, 2)).reshape(group_count * token_count, width)
    gradient = lax.dot_general(
        columns, context, (((0,), (0,)), ((), ())), preferred_element_type=jnp.float32
    )
    moment_one = beta_first * first_moment[0] + (1.0 - beta_first) * gradient
    moment_two = beta_second * second_moment[0] + (1.0 - beta_second) * gradient * gradient
    bias_first = 1.0 - beta_first**100.0
    bias_second = 1.0 - beta_second**100.0
    step_size = moment_one / bias_first / (jnp.sqrt(moment_two / bias_second) + epsilon)
    weight_float = out_proj[0].astype(jnp.float32)
    updated = (weight_float - learn_rate * (step_size + decay_rate * weight_float)).astype(
        jnp.bfloat16
    )
    payload = jnp.concatenate(
        [updated, moment_one.astype(jnp.bfloat16), moment_two.astype(jnp.bfloat16)], axis=0
    )
    own_member = lax.axis_index("member")
    index = lax.iota(jnp.int32, member_count)
    goes_up = jnp.logical_and(copy_flag == 1, donor_index < index)
    goes_down = jnp.logical_and(copy_flag == 1, donor_index > index)
    until = index[:, None] >= index[None, :]
    up_rank = jnp.sum(jnp.logical_and(until, goes_up[None]).astype(jnp.int32), axis=1)
    down_rank = jnp.sum(jnp.logical_and(until, goes_down[None]).astype(jnp.int32), axis=1)
    rounds = jnp.maximum(jnp.max(up_rank), jnp.max(down_rank))

    def one_round(state):
        number, held = state
        up_now = jnp.logical_and(goes_up, up_rank == number + 1)
        down_now = jnp.logical_and(goes_down, down_rank == number + 1)
        mine = index == own_member
        from_me = donor_index == own_member
        flags = jnp.stack(
            [
                jnp.any(jnp.logical_and(up_now, from_me)),
                jnp.any(jnp.logical_and(down_now, from_me)),
                jnp.any(jnp.logical_and(up_now, mine)),
                jnp.any(jnp.logical_and(down_now, mine)),
            ]
        ).astype(jnp.int32)
        return number + 1, chain(flags, held, member_count)

    chosen = lax.while_loop(lambda state: state[0] < rounds, one_round, (jnp.int32(0), payload))[1]
    taken_weight = chosen[:row_count]
    flagged = jnp.any(jnp.logical_and(copy_flag == 1, index == own_member))
    perturbed = (taken_weight.astype(jnp.float32) + explore_noise[0].astype(jnp.float32)).astype(
        jnp.bfloat16
    )
    new_proj = jnp.where(flagged, perturbed, taken_weight)
    new_first = chosen[row_count : 2 * row_count].astype(jnp.float32)
    new_second = chosen[2 * row_count :].astype(jnp.float32)
    return (new_proj[None], new_first[None], new_second[None])


def solution(mesh):
    return jax.shard_map(
        body,
        mesh=mesh,
        in_specs=(
            P("member", "fsdp", None, None),
            P("member", "fsdp", None, None),
            P("member", "fsdp", None, None),
            P("member", "fsdp", None),
            P("member", "fsdp", None),
            P("member", "fsdp", None),
            P("member", "fsdp", None),
            P("member", "fsdp", None),
            P(),
            P(),
        ),
        out_specs=(P("member", "fsdp", None), P("member", "fsdp", None), P("member", "fsdp", None)),
        check_vma=False,
    )
```

time: 759 us -> 330 us (0.43)
  waiting for transfers between devices: 368 us -> 51.7 us
  blocking collectives: 204 us -> 0 us
  Pallas kernels: 0 us -> 173 us
  local copies, waits for them, and re-layouts: 68 us -> 23.5 us
  starting transfers between devices: 34.6 us -> 8.86 us
  other arithmetic: 47.1 us -> 39.3 us
    all_to_all x8 -> x2, waiting for transfers between devices: 359 us -> 34.3 us  [the longest x1 19.2 us: body(): lax.all_to_all(stacked, 'fsdp', split_axis=0, concat_axis=0, tiled=True)]
    all_to_all x3 -> x0, blocking collectives: 204 us -> none  [the longest x1 97.3 us: body(): lax.all_to_all(shortened(chosen_second), 'member', split_axis=0, concat_a...]
    pallas_call x0 -> x1, Pallas kernels: none -> 173 us  [chain(): pl.pallas_call(functools.partial(chain_kernel, size, chunks), out_shape=j...]
    all_to_all x8 -> x2, starting transfers between devices: 34.5 us -> 8.86 us  [the longest x1 5.16 us: body(): lax.all_to_all(stacked, 'fsdp', split_axis=0, concat_axis=0, tiled=True)]
    unnamed x25 -> x10, local copies, waits for them, and re-layouts: 31.3 us -> 5.71 us
    convert_element_type x2 -> x1, other arithmetic: 25.7 us -> 2.62 us  [one_round(): flags = jnp.stack([jnp.any(jnp.logical_and(up_now, from_me)), jnp.any(jnp...]
    concatenate x0 -> x1, other arithmetic: none -> 18.1 us  [body(): jnp.concatenate([updated, moment_one.astype(jnp.bfloat16), moment_two.ast...]
    gather x3 -> x0, local copies, waits for them, and re-layouts: 15 us -> none  [the longest x1 5.01 us: body(): chosen_second = jnp.take(second_slices, source, axis=0)]
  transfers between devices with their start and end apart: 9 -> 3, of which waited for: 8 -> 3; matrix products, arithmetic and copies ran while one was open for 8% -> 1% of each run, Pallas kernels for 0% -> 0%
where the time goes in v1:
time: 330 us; the launch traced here: 329 us
  Pallas kernels  173 us (52%)
  waiting for transfers between devices  51.7 us (16%)
  other arithmetic  39.3 us (12%)
  local copies, waits for them, and re-layouts  23.5 us (7%)
  matrix products  17.3 us (5%)
  between operations  15.4 us (5%)
  starting transfers between devices  8.86 us (3%)
    pallas_call x1, Pallas kernels, chain(): pl.pallas_call(functools.partial(chain_kernel, size, chunks), out_shape=j...  173 us
    all_to_all x1, waiting for transfers between devices, body(): lax.all_to_all(stacked, 'fsdp', split_axis=0, concat_axis=0, tiled=True)  19.2 us
    concatenate x1, other arithmetic, body(): jnp.concatenate([updated, moment_one.astype(jnp.bfloat16), moment_two.ast...  18.1 us
    all_gather x1, waiting for transfers between devices, body(): context = lax.all_gather(context, 'fsdp', axis=0)  17.3 us
    dot_general x1, matrix products, body(): lax.dot_general(columns, context, (((0,), (0,)), ((), ())), preferred_ele...  16.1 us
    all_to_all x1, waiting for transfers between devices, body(): lax.all_to_all(columns, 'fsdp', split_axis=0, concat_axis=0, tiled=True)  15.2 us
    broadcast_in_dim x1, other arithmetic, body(): return (new_proj[None], new_first[None], new_second[None])  13.2 us
    while x1, local copies, waits for them, and re-layouts  10.7 us
  transfers between devices with their start and end apart: 3, of which 3 were waited for; matrix products, arithmetic and copies ran while one was open for 1% of the time, Pallas kernels for 0%

profile of v1, /device:TPU:0, one launch (start us, length us, event | category | flops | bytes accessed | tf_op | source)
XLA Modules:
  0.0 329.0 jit_solution(226598334763868756)
XLA Ops:
  7.2 1.5 copy.52
  8.6 1.5 copy.53
  10.1 1.5 copy.54
  11.6 0.2 maximum_bitcast_fusion
  11.7 1.6 copy.55
  13.3 5.2 %all-to-all-start = ((bf16[4,3,128,512]{3,2,1,0:T(8,128)(2,1)}), bf16[4,3,128,512]{3,2,1,0:T(8,128)(2,1)S(1)}, u32[]{:S(2)}, u32[]{:S(2)}) async-start(bf16[4,3,128,512]{3,2,1,0:T(8,128)(2,1)} %copy.55), calls=%async_computation | async-start | bytes 3145728 | tf_op jit(solution)/shard_map/all_to_all | solution.py:161
  18.5 0.0 all-gather.2.cloned.1.call-start
  18.5 0.1 iota_compare_fusion
  18.6 19.2 %all-to-all-done = bf16[4,3,128,512]{3,2,1,0:T(8,128)(2,1)S(1)} async-done(((bf16[4,3,128,512]{3,2,1,0:T(8,128)(2,1)}), bf16[4,3,128,512]{3,2,1,0:T(8,128)(2,1)S(1)}, u32[]{:S(2)}, u32[]{:S(2)}) %all-to-all-start) | async-done | bytes 1572896 | tf_op jit(solution)/shard_map/all_to_all | solution.py:161
  37.7 0.1 fusion.36
  37.8 0.1 reshape.49
  38.0 0.1 squeeze.15
  38.1 0.1 squeeze.14
  38.2 0.7 fusion.29
  38.9 2.4 fusion.37
  41.3 0.0 copy-start
  41.3 0.5 fusion.25
  41.8 0.0 copy-start.1
  41.9 0.0 copy-start.2
  41.9 1.0 copy.60
  42.9 0.0 all-gather.2.cloned.1.call-update
  42.9 0.0 copy-done
  42.9 1.3 copy.62
  44.2 3.7 %all-to-all-start.1 = ((bf16[4,128,1024]{1,2,0:T(8,128)(2,1)}), bf16[4,128,1024]{1,2,0:T(8,128)(2,1)S(1)}, u32[]{:S(2)}, u32[]{:S(2)}) async-start(bf16[4,128,1024]{1,2,0:T(8,128)(2,1)} %bitcast.13), calls=%async_computation.1 | async-start | bytes 2097152 | tf_op jit(solution)/shard_map/all_to_all | solution.py:162
  47.9 0.0 copy-done.1
  47.9 0.0 copy-done.2
  47.9 0.6 compare_and_fusion.2
  48.6 0.2 convert_reduce_fusion
  48.7 0.6 reduce_max.28
  49.4 0.6 reduce_max.29
  51.2 15.2 %all-to-all-done.1 = bf16[4,128,1024]{1,2,0:T(8,128)(2,1)S(1)} async-done(((bf16[4,128,1024]{1,2,0:T(8,128)(2,1)}), bf16[4,128,1024]{1,2,0:T(8,128)(2,1)S(1)}, u32[]{:S(2)}, u32[]{:S(2)}) %all-to-all-start.1) | async-done | bytes 1048608 | tf_op jit(solution)/shard_map/all_to_all | solution.py:162
  66.4 1.3 copy.63
  67.7 17.3 %all-gather.2.cloned.1.call-done = bf16[4,512,512]{2,1,0:T(8,128)(2,1)} async-done(((bf16[1,512,512]{2,1,0:T(8,128)(2,1)}), bf16[4,512,512]{2,1,0:T(8,128)(2,1)}) %all-gather.2.cloned.1.call-update) | async-done | bytes 2097168 | tf_op jit(solution)/shard_map/all_gather | solution.py:168
  85.1 2.8 copy.61
  87.8 16.1 %fusion.5 = (bf16[1024,2048]{1,0:T(8,128)(2,1)S(1)}, bf16[1024,2048]{1,0:T(8,128)(2,1)S(1)}, bf16[1024,2048]{1,0:T(8,128)(2,1)}) fusion(bf16[1,1024,2048]{2,1,0:T(8,128)(2,1)} %param.16, f32[1,1024,2048]{2,1,0:T(8,128)} %param.17, f32[1,1024,2048]{2,1,0:T(8,128)} %param.18, bf16[512,2048]{0,1:T(8,128)(2,1)S(1)} %bitcast.88, bf16[512,1024]{1,0:T(8,128)(2,1)} %bitcast.92), kind=kOutput, calls=%fused_computation.15 | convolution fusion | flops 2187329536 | bytes 36700160 | tf_op jit(solution)/shard_map/dot_general | solution.py:170
  103.9 18.1 %pad_maximum_fusion = bf16[3072,2048]{1,0:T(8,128)(2,1)} fusion(bf16[1024,2048]{1,0:T(8,128)(2,1)} %get-tuple-element.104, bf16[1024,2048]{1,0:T(8,128)(2,1)S(1)} %get-tuple-element.103, bf16[1024,2048]{1,0:T(8,128)(2,1)S(1)} %get-tuple-element.102), kind=kLoop, calls=%fused_computation.9 | loop fusion | flops 37748736 | bytes 25165824 | tf_op jit(solution)/shard_map/concatenate | solution.py:182
  122.0 186.9 %while.11 = (s32[]{:T(128)}, bf16[3072,2048]{1,0:T(8,128)(2,1)}, s32[]{:T(128)}, s32[8]{0:T(128)S(1)}, pred[8]{0:T(512)(128)(4,1)S(1)}, /*index=5*/s32[]{:T(128)...) while((s32[]{:T(128)}, bf16[3072,2048]{1,0:T(8,128)(2,1)}, s32[]{:T(128)}, ...), condition=%wide.region_12.13_spmd.clone, body=%wide.region_7.12_spmd.clone.sunk | while | flops 126 | bytes 25166068 | solution.py:210
  122.0 10.7 %copy.81.own_hbm = bf16[3072,2048]{1,0:T(8,128)(2,1)} copy(bf16[3072,2048]{1,0:T(8,128)(2,1)} %get-tuple-element.195) | data formatting | bytes 25165824 | tf_op jit(solution)/shard_map/while
  132.7 0.7 and_reduce_fusion.6
  133.4 2.6 add_convert_fusion.2.flags
  136.0 172.8 %body.1 = bf16[3072,2048]{1,0:T(8,128)(2,1)} custom-call(s32[4]{0:T(128)S(1)} %add_convert_fusion.2.flags, bf16[3072,2048]{1,0:T(8,128)(2,1)} %copy.81.own_hbm), custom_call_target="tpu_custom_call" | custom-call | tf_op jit(solution)/shard_map/while/body/pallas_call | solution.py:103
  308.9 13.2 %bitcast_convert_fusion = (f32[1,1024,2048]{2,1,0:T(8,128)}, f32[1,1024,2048]{2,1,0:T(8,128)}, bf16[1,1024,2048]{2,1,0:T(8,128)(2,1)}) fusion(bf16[3072,2048]{1,0:T(8,128)(2,1)} %get-tuple-element.56, bf16[1,1024,2048]{2,1,0:T(8,128)(2,1)} %param.19, pred[]{:T(512)} %get-tuple-element.113), kind=kLoop, calls=%fused_computation.23 | loop fusion | flops 14680064 | bytes 37748736 | tf_op jit(solution)/shard_map/broadcast_in_dim | solution.py:219
Async XLA Ops:
  13.3 24.4 %all-to-all-start = ((bf16[4,3,128,512]{3,2,1,0:T(8,128)(2,1)}), bf16[4,3,128,512]{3,2,1,0:T(8,128)(2,1)S(1)}, u32[]{:S(2)}, u32[]{:S(2)}) async-start(bf16[4,3,128,512]{3,2,1,0:T(8,128)(2,1)} %copy.55), calls=%async_computation | async-start | bytes 3145728 | tf_op jit(solution)/shard_map/all_to_all | solution.py:161
  18.5 66.6 %all-gather.2.cloned.1.call-start = ((), (), s32[]{:S(2)}) async-start(), calls=%async_computation.2 | async-start | bytes 2621440 | tf_op jit(solution)/shard_map/all_gather | solution.py:168
  41.3 1.6 copy-start
  41.8 6.1 %copy-start.1 = (s32[8]{0:T(128)S(1)}, s32[8]{0:T(128)}, u32[]{:S(2)}) copy-start(s32[8]{0:T(128)} %param.20) | copy-start | bytes 100
  41.9 6.1 %copy-start.2 = (s32[8]{0:T(128)S(1)}, s32[8]{0:T(128)}, u32[]{:S(2)}) copy-start(s32[8]{0:T(128)} %param.21) | copy-start | bytes 100
  44.2 22.2 %all-to-all-start.1 = ((bf16[4,128,1024]{1,2,0:T(8,128)(2,1)}), bf16[4,128,1024]{1,2,0:T(8,128)(2,1)S(1)}, u32[]{:S(2)}, u32[]{:S(2)}) async-start(bf16[4,128,1024]{1,2,0:T(8,128)(2,1)} %bitcast.13), calls=%async_computation.1 | async-start | bytes 2097152 | tf_op jit(solution)/shard_map/all_to_all | solution.py:162
Sparse Core Ops, SparseCore 0:
  43.0 41.9 all-gather.1

commit v2 on v1

--- a/solution.py
+++ b/solution.py
@@ -18,11 +18,16 @@
 MESH = pl.DeviceIdType.MESH
 
 
-def chain_kernel(size, chunks, flags, own_hbm, out_hbm, own, up, down, up_send, up_recv, down_send, down_recv, local_sem):
+def chain_kernel(size, chunks, flags, one_in, two_in, three_in, one_out, two_out, three_out, own, up, down, up_send, up_recv, down_send, down_recv, local_sem):
     me = lax.axis_index("member")
     last = size - 1
-    load = pltpu.make_async_copy(own_hbm, own, local_sem)
-    load.start()
+    length = one_in.shape[0]
+    loads = [
+        pltpu.make_async_copy(ref, own.at[pl.ds(place * length, length)], local_sem.at[place])
+        for place, ref in enumerate((one_in, two_in, three_in))
+    ]
+    for load in loads:
+        load.start()
     barrier = pltpu.get_barrier_semaphore()
 
     @pl.when(me > 0)
@@ -41,7 +46,8 @@
     def _():
         pl.semaphore_wait(barrier, 2)
 
-    load.wait()
+    for load in loads:
+        load.wait()
 
     def rows(chunk):
         return pl.ds(pl.multiple_of(chunk * chunk_rows, chunk_rows), chunk_rows)
@@ -80,38 +86,84 @@
         advance(step - lag * me, up, up_send, up_recv, me == 0, me == last, above, flags[0])
         advance(step - lag * (last - me), down, down_send, down_recv, me == last, me == 0, below, flags[1])
 
-    @pl.loop(0, chunks)
-    def _(chunk):
-        @pl.when(me < last)
-        def _():
-            copy(up, up_send, up_recv, chunk, above).wait_send()
-
-        @pl.when(me > 0)
-        def _():
-            copy(down, down_send, down_recv, chunk, below).wait_send()
-
-        part = lax.select(flags[2] == 1, up[rows(chunk), :], own[rows(chunk), :])
-        own[rows(chunk), :] = lax.select(flags[3] == 1, down[rows(chunk), :], part)
-
-    store = pltpu.make_async_copy(own, out_hbm, local_sem)
-    store.start()
-    store.wait()
+    stores = [
+        pltpu.make_async_copy(own.at[pl.ds(place * length, length)], ref, local_sem.at[place])
+        for place, ref in enumerate((one_out, two_out, three_out))
+    ]
+    each = length // chunk_rows
+    for place, store in enumerate(stores):
+
+        @pl.loop(place * each, (place + 1) * each)
+        def _(chunk):
+            @pl.when(me < last)
+            def _():
+                copy(up, up_send, up_recv, chunk, above).wait_send()
+
+            @pl.when(me > 0)
+            def _():
+                copy(down, down_send, down_recv, chunk, below).wait_send()
+
+            part = lax.select(flags[2] == 1, up[rows(chunk), :], own[rows(chunk), :])
+            own[rows(chunk), :] = lax.select(flags[3] == 1, down[rows(chunk), :], part)
+
+        store.start()
+    for store in stores:
+        store.wait()
 
 
 def chain(flags, payload, size):
-    chunks = payload.shape[0] // chunk_rows
+    length, width = payload[0].shape
+    kind = payload[0].dtype
+    chunks = len(payload) * length // chunk_rows
     return pl.pallas_call(
         functools.partial(chain_kernel, size, chunks),
-        out_shape=jax.ShapeDtypeStruct(payload.shape, payload.dtype),
-        in_specs=[pl.BlockSpec(memory_space=pltpu.SMEM), pl.BlockSpec(memory_space=pl.ANY)],
-        out_specs=pl.BlockSpec(memory_space=pl.ANY),
-        scratch_shapes=[pltpu.VMEM(payload.shape, payload.dtype) for _ in range(3)]
+        out_shape=[jax.ShapeDtypeStruct((length, width), kind) for _ in payload],
+        in_specs=[pl.BlockSpec(memory_space=pltpu.SMEM)]
+        + [pl.BlockSpec(memory_space=pl.ANY) for _ in payload],
+        out_specs=[pl.BlockSpec(memory_space=pl.ANY) for _ in payload],
+        scratch_shapes=[pltpu.VMEM((len(payload) * length, width), kind) for _ in range(3)]
         + [pltpu.SemaphoreType.DMA((chunks,)) for _ in range(4)]
-        + [pltpu.SemaphoreType.DMA],
+        + [pltpu.SemaphoreType.DMA((len(payload),))],
+        input_output_aliases={place + 1: place for place in range(len(payload))},
         compiler_params=pltpu.CompilerParams(
             collective_id=0, has_side_effects=True, vmem_limit_bytes=48 * 2**20
         ),
-    )(flags, payload)
+    )(flags, *payload)
+
+
+def step_kernel(grad_ref, context_ref, weight_ref, first_ref, second_ref, new_weight, new_first, new_second):
+    gradient = jnp.dot(grad_ref[...], context_ref[...], preferred_element_type=jnp.float32)
+    moment_one = beta_first * first_ref[...] + (1.0 - beta_first) * gradient
+    moment_two = beta_second * second_ref[...] + (1.0 - beta_second) * gradient * gradient
+    bias_first = 1.0 - beta_first**100.0
+    bias_second = 1.0 - beta_second**100.0
+    step_size = moment_one / bias_first / (jnp.sqrt(moment_two / bias_second) + epsilon)
+    weight = weight_ref[...].astype(jnp.float32)
+    updated = weight - learn_rate * (step_size + decay_rate * weight)
+    new_weight[...] = updated.astype(new_weight.dtype)
+    new_first[...] = moment_one.astype(new_first.dtype)
+    new_second[...] = moment_two.astype(new_second.dtype)
+
+
+def member_step(grad_columns, context, weight, first, second):
+    rows, width = weight.shape
+    tokens = context.shape[0]
+    tile = 128
+    wide = pl.BlockSpec((tile, width), lambda i: (i, 0))
+    return pl.pallas_call(
+        step_kernel,
+        grid=(rows // tile,),
+        out_shape=[jax.ShapeDtypeStruct((rows, width), jnp.bfloat16) for _ in range(3)],
+        in_specs=[
+            pl.BlockSpec((tile, tokens), lambda i: (i, 0)),
+            pl.BlockSpec((tokens, width), lambda i: (0, 0)),
+            wide,
+            wide,
+            wide,
+        ],
+        out_specs=[wide, wide, wide],
+        compiler_params=pltpu.CompilerParams(vmem_limit_bytes=48 * 2**20),
+    )(grad_columns, context, weight, first, second)
 
 
 def group_attention(queries, keys, values):
@@ -167,20 +219,8 @@
     context = group_attention(heads[0], heads[1], heads[2])
     context = lax.all_gather(context, "fsdp", axis=0)
     context = jnp.transpose(context, (1, 0, 2)).reshape(group_count * token_count, width)
-    gradient = lax.dot_general(
-        columns, context, (((0,), (0,)), ((), ())), preferred_element_type=jnp.float32
-    )
-    moment_one = beta_first * first_moment[0] + (1.0 - beta_first) * gradient
-    moment_two = beta_second * second_moment[0] + (1.0 - beta_second) * gradient * gradient
-    bias_first = 1.0 - beta_first**100.0
-    bias_second = 1.0 - beta_second**100.0
-    step_size = moment_one / bias_first / (jnp.sqrt(moment_two / bias_second) + epsilon)
-    weight_float = out_proj[0].astype(jnp.float32)
-    updated = (weight_float - learn_rate * (step_size + decay_rate * weight_float)).astype(
-        jnp.bfloat16
-    )
-    payload = jnp.concatenate(
-        [updated, moment_one.astype(jnp.bfloat16), moment_two.astype(jnp.bfloat16)], axis=0
+    payload = tuple(
+        member_step(columns.T, context, out_proj[0], first_moment[0], second_moment[0])
     )
     own_member = lax.axis_index("member")
     index = lax.iota(jnp.int32, member_count)
@@ -205,17 +245,17 @@
                 jnp.any(jnp.logical_and(down_now, mine)),
             ]
         ).astype(jnp.int32)
-        return number + 1, chain(flags, held, member_count)
+        return number + 1, tuple(chain(flags, held, member_count))
 
     chosen = lax.while_loop(lambda state: state[0] < rounds, one_round, (jnp.int32(0), payload))[1]
-    taken_weight = chosen[:row_count]
+    taken_weight, taken_first, taken_second = chosen
     flagged = jnp.any(jnp.logical_and(copy_flag == 1, index == own_member))
     perturbed = (taken_weight.astype(jnp.float32) + explore_noise[0].astype(jnp.float32)).astype(
         jnp.bfloat16
     )
     new_proj = jnp.where(flagged, perturbed, taken_weight)
-    new_first = chosen[row_count : 2 * row_count].astype(jnp.float32)
-    new_second = chosen[2 * row_count :].astype(jnp.float32)
+    new_first = taken_first.astype(jnp.float32)
+    new_second = taken_second.astype(jnp.float32)
     return (new_proj[None], new_first[None], new_second[None])
 
 

time: 330 us -> 305 us (0.924)
  matrix products: 17.3 us -> 1.21 us
  Pallas kernels: 173 us -> 188 us
  other arithmetic: 39.3 us -> 25 us
  local copies, waits for them, and re-layouts: 23.5 us -> 11.9 us
    concatenate x1 -> x0, other arithmetic: 18.1 us -> none  [body(): jnp.concatenate([updated, moment_one.astype(jnp.bfloat16), moment_two.ast...]
    dot_general x1 -> x0, matrix products: 16.1 us -> none  [body(): lax.dot_general(columns, context, (((0,), (0,)), ((), ())), preferred_ele...]
    pallas_call x1 -> x2, Pallas kernels: 173 us -> 188 us  [the longest x1 172 us: chain(): pl.pallas_call(functools.partial(chain_kernel, size, chunks), out_shape=[...]
    while x1 -> x0, local copies, waits for them, and re-layouts: 10.7 us -> none
    broadcast_in_dim x1 -> x3, other arithmetic: 13.2 us -> 16.8 us  [body(): return (new_proj[None], new_first[None], new_second[None])]
    unnamed x10 -> x16, local copies, waits for them, and re-layouts: 5.71 us -> 6.9 us
where the time goes in v2:
time: 305 us; the launch traced here: 304 us
  Pallas kernels  188 us (62%)
  waiting for transfers between devices  53.9 us (18%)
  other arithmetic  25 us (8%)
  between operations  15.4 us (5%)
  local copies, waits for them, and re-layouts  11.9 us (4%)
  starting transfers between devices  8.68 us (3%)
    pallas_call x1, Pallas kernels, chain(): pl.pallas_call(functools.partial(chain_kernel, size, chunks), out_shape=[...  172 us
    all_gather x1, waiting for transfers between devices, body(): context = lax.all_gather(context, 'fsdp', axis=0)  19.4 us
    all_to_all x1, waiting for transfers between devices, body(): lax.all_to_all(stacked, 'fsdp', split_axis=0, concat_axis=0, tiled=True)  19.2 us
    broadcast_in_dim x3, other arithmetic, body(): return (new_proj[None], new_first[None], new_second[None])  16.8 us
    pallas_call x1, Pallas kernels, member_step(): pl.pallas_call(step_kernel, grid=(rows // tile,), out_shape=[jax.ShapeDty...  16.6 us
    all_to_all x1, waiting for transfers between devices, body(): lax.all_to_all(columns, 'fsdp', split_axis=0, concat_axis=0, tiled=True)  15.3 us
    unnamed x16, local copies, waits for them, and re-layouts  6.9 us
  transfers between devices with their start and end apart: 3, of which 3 were waited for; matrix products, arithmetic and copies ran while one was open for 1% of the time, Pallas kernels for 0%

profile of v2, /device:TPU:0, one launch (start us, length us, event | category | flops | bytes accessed | tf_op | source)
XLA Modules:
  0.0 304.5 jit_solution(16928805250516301687)
XLA Ops:
  7.2 1.5 copy.53
  8.6 1.5 copy.54
  10.1 1.5 copy.55
  11.6 0.2 maximum_bitcast_fusion
  11.7 1.6 copy.56
  13.3 5.2 %all-to-all-start.1 = ((bf16[4,3,128,512]{3,2,1,0:T(8,128)(2,1)}), bf16[4,3,128,512]{3,2,1,0:T(8,128)(2,1)S(1)}, u32[]{:S(2)}, u32[]{:S(2)}) async-start(bf16[4,3,128,512]{3,2,1,0:T(8,128)(2,1)} %copy.56), calls=%async_computation.1 | async-start | bytes 3145728 | tf_op jit(solution)/shard_map/all_to_all | solution.py:213
  18.5 0.0 all-gather.2.cloned.1.call-start
  18.5 0.1 iota_compare_fusion
  18.6 19.2 %all-to-all-done.1 = bf16[4,3,128,512]{3,2,1,0:T(8,128)(2,1)S(1)} async-done(((bf16[4,3,128,512]{3,2,1,0:T(8,128)(2,1)}), bf16[4,3,128,512]{3,2,1,0:T(8,128)(2,1)S(1)}, u32[]{:S(2)}, u32[]{:S(2)}) %all-to-all-start.1) | async-done | bytes 1572896 | tf_op jit(solution)/shard_map/all_to_all | solution.py:213
  37.7 0.1 fusion.29
  37.8 0.1 reshape.42
  38.0 0.1 squeeze.21
  38.1 0.1 squeeze.20
  38.2 0.7 fusion.22
  38.9 2.4 fusion.30
  41.3 0.0 copy-start.3
  41.3 0.5 fusion.18
  41.8 0.0 copy-start.4
  41.9 0.0 copy-start.5
  41.9 1.0 copy.61
  42.9 0.0 all-gather.2.cloned.1.call-update
  42.9 0.0 copy-done.3
  42.9 1.3 copy.51
  44.2 3.5 %all-to-all-start = ((bf16[4,128,1024]{1,2,0:T(8,128)(2,1)}), bf16[4,128,1024]{1,2,0:T(8,128)(2,1)S(1)}, u32[]{:S(2)}, u32[]{:S(2)}) async-start(bf16[4,128,1024]{1,2,0:T(8,128)(2,1)} %bitcast.1), calls=%async_computation | async-start | bytes 2097152 | tf_op jit(solution)/shard_map/all_to_all | solution.py:214
  47.7 0.0 copy-done.4
  47.8 0.0 copy-done.5
  47.8 0.7 compare_and_fusion.2
  48.4 0.1 convert_reduce_fusion
  48.6 0.7 reduce_max.28
  49.3 0.6 reduce_max.29
  51.1 15.3 %all-to-all-done = bf16[4,128,1024]{1,2,0:T(8,128)(2,1)S(1)} async-done(((bf16[4,128,1024]{1,2,0:T(8,128)(2,1)}), bf16[4,128,1024]{1,2,0:T(8,128)(2,1)S(1)}, u32[]{:S(2)}, u32[]{:S(2)}) %all-to-all-start) | async-done | bytes 1048608 | tf_op jit(solution)/shard_map/all_to_all | solution.py:214
  66.4 0.1 bitcast_bitcast_fusion.grad_ref
  66.5 19.4 %all-gather.2.cloned.1.call-done = bf16[4,512,512]{2,1,0:T(8,128)(2,1)} async-done(((bf16[1,512,512]{2,1,0:T(8,128)(2,1)}), bf16[4,512,512]{2,1,0:T(8,128)(2,1)}) %all-gather.2.cloned.1.call-update) | async-done | bytes 2097168 | tf_op jit(solution)/shard_map/all_gather | solution.py:220
  86.0 1.9 copy.66
  87.9 16.6 %shard_map.121 = (bf16[1024,2048]{1,0:T(8,128)(2,1)}, bf16[1024,2048]{1,0:T(8,128)(2,1)}, bf16[1024,2048]{1,0:T(8,128)(2,1)}) custom-call(bf16[1024,512]{1,0:T(8,128)(2,1)S(1)} %bitcast_bitcast_fusion.grad_ref, bf16[512,2048]{1,0:T(8,128)(2,1)S(1)} %bitcast.66, bf16[1024,2048]{1,0:T(8,128)(2,1)} %bitcast.70, f32[1024,2048]{1,0:T(8,128)} %bitcast.67, ...), custom_call_target="tpu_custom_call" | custom-call | tf_op jit(solution)/shard_map/pallas_call | solution.py:153
  104.5 175.2 %while.15 = (s32[]{:T(128)}, bf16[1024,2048]{1,0:T(8,128)(2,1)}, bf16[1024,2048]{1,0:T(8,128)(2,1)}, bf16[1024,2048]{1,0:T(8,128)(2,1)}, s32[]{:T(128)}, /*index...) while((s32[]{:T(128)}, bf16[1024,2048]{1,0:T(8,128)(2,1)}, ...), condition=%wide.region_12.13_spmd.clone, body=%wide.region_7.12_spmd.clone.sunk | while | flops 126 | bytes 261 | solution.py:250
  104.5 0.8 and_reduce_fusion.6
  105.2 2.7 add_convert_fusion.2.flags
  107.9 171.5 %body.1 = (bf16[1024,2048]{1,0:T(8,128)(2,1)}, bf16[1024,2048]{1,0:T(8,128)(2,1)}, bf16[1024,2048]{1,0:T(8,128)(2,1)}) custom-call(s32[4]{0:T(128)S(1)} %add_convert_fusion.2.flags, bf16[1024,2048]{1,0:T(8,128)(2,1)} %get-tuple-element.243.one_in, ...), custom_call_target="tpu_custom_call", output_to_operand_aliasing={{0}: (1, {}), {1}: (2, {}), {2}: (3, {})} | custom-call | tf_op jit(solution)/shard_map/while/body/pallas_call | solution.py:118
  279.6 0.0 copy-start.1
  279.6 6.8 %bitcast_convert_fusion = f32[1,1024,2048]{2,1,0:T(8,128)} fusion(bf16[1024,2048]{1,0:T(8,128)(2,1)} %get-tuple-element.79), kind=kLoop, calls=%fused_computation.13 | loop fusion | flops 2097152 | bytes 12582912 | tf_op jit(solution)/shard_map/broadcast_in_dim | solution.py:259
  286.4 0.0 copy-done.1
  286.4 0.0 copy-start
  286.4 0.0 copy-start.2
  286.4 5.3 %bitcast_convert_fusion.1 = f32[1,1024,2048]{2,1,0:T(8,128)} fusion(bf16[1024,2048]{1,0:T(8,128)(2,1)S(1)} %copy-done.1), kind=kLoop, calls=%fused_computation.14 | loop fusion | flops 2097152 | bytes 12582912 | tf_op jit(solution)/shard_map/broadcast_in_dim | solution.py:259
  291.8 0.0 copy-done
  291.8 1.2 copy-done.2
  292.9 4.7 %fusion.5 = bf16[1,1024,2048]{2,1,0:T(8,128)(2,1)} fusion(bf16[1024,2048]{1,0:T(8,128)(2,1)S(1)} %copy-done, bf16[1,1024,2048]{2,1,0:T(8,128)(2,1)S(1)} %copy-done.2, pred[]{:T(512)} %get-tuple-element.141), kind=kLoop, calls=%fused_computation.12 | loop fusion | flops 10485760 | bytes 12582913 | tf_op jit(solution)/shard_map/broadcast_in_dim | solution.py:259
Async XLA Ops:
  13.3 24.4 %all-to-all-start.1 = ((bf16[4,3,128,512]{3,2,1,0:T(8,128)(2,1)}), bf16[4,3,128,512]{3,2,1,0:T(8,128)(2,1)S(1)}, u32[]{:S(2)}, u32[]{:S(2)}) async-start(bf16[4,3,128,512]{3,2,1,0:T(8,128)(2,1)} %copy.56), calls=%async_computation.1 | async-start | bytes 3145728 | tf_op jit(solution)/shard_map/all_to_all | solution.py:213
  18.5 67.5 %all-gather.2.cloned.1.call-start = ((), (), s32[]{:S(2)}) async-start(), calls=%async_computation.2 | async-start | bytes 2621440 | tf_op jit(solution)/shard_map/all_gather | solution.py:220
  41.3 1.6 copy-start.3
  41.8 5.9 %copy-start.4 = (s32[8]{0:T(128)S(1)}, s32[8]{0:T(128)}, u32[]{:S(2)}) copy-start(s32[8]{0:T(128)} %param.20) | copy-start | bytes 100
  41.9 5.9 %copy-start.5 = (s32[8]{0:T(128)S(1)}, s32[8]{0:T(128)}, u32[]{:S(2)}) copy-start(s32[8]{0:T(128)} %param.21) | copy-start | bytes 100
  44.2 22.2 %all-to-all-start = ((bf16[4,128,1024]{1,2,0:T(8,128)(2,1)}), bf16[4,128,1024]{1,2,0:T(8,128)(2,1)S(1)}, u32[]{:S(2)}, u32[]{:S(2)}) async-start(bf16[4,128,1024]{1,2,0:T(8,128)(2,1)} %bitcast.1), calls=%async_computation | async-start | bytes 2097152 | tf_op jit(solution)/shard_map/all_to_all | solution.py:214
  279.6 6.8 %copy-start.1 = (bf16[1024,2048]{1,0:T(8,128)(2,1)S(1)}, bf16[1024,2048]{1,0:T(8,128)(2,1)}, u32[]{:S(2)}) copy-start(bf16[1024,2048]{1,0:T(8,128)(2,1)} %get-tuple-element.78) | copy-start | bytes 12582916
  286.4 5.3 %copy-start = (bf16[1024,2048]{1,0:T(8,128)(2,1)S(1)}, bf16[1024,2048]{1,0:T(8,128)(2,1)}, u32[]{:S(2)}) copy-start(bf16[1024,2048]{1,0:T(8,128)(2,1)} %get-tuple-element.77) | copy-start | bytes 12582916
  286.4 6.5 %copy-start.2 = (bf16[1,1024,2048]{2,1,0:T(8,128)(2,1)S(1)}, bf16[1,1024,2048]{2,1,0:T(8,128)(2,1)}, u32[]{:S(2)}) copy-start(bf16[1,1024,2048]{2,1,0:T(8,128)(2,1)} %param.19) | copy-start | bytes 12582916
Sparse Core Ops, SparseCore 0:
  43.0 42.8 all-gather.1

commit v3 on v2

--- a/solution.py
+++ b/solution.py
@@ -81,32 +81,36 @@
     above = lax.rem(me + 1, size)
     below = lax.rem(me + size - 1, size)
 
-    @pl.loop(0, chunks + lag * last)
-    def _(step):
-        advance(step - lag * me, up, up_send, up_recv, me == 0, me == last, above, flags[0])
-        advance(step - lag * (last - me), down, down_send, down_recv, me == last, me == 0, below, flags[1])
-
     stores = [
         pltpu.make_async_copy(own.at[pl.ds(place * length, length)], ref, local_sem.at[place])
         for place, ref in enumerate((one_out, two_out, three_out))
     ]
     each = length // chunk_rows
-    for place, store in enumerate(stores):
-
-        @pl.loop(place * each, (place + 1) * each)
-        def _(chunk):
-            @pl.when(me < last)
-            def _():
-                copy(up, up_send, up_recv, chunk, above).wait_send()
-
-            @pl.when(me > 0)
-            def _():
-                copy(down, down_send, down_recv, chunk, below).wait_send()
-
-            part = lax.select(flags[2] == 1, up[rows(chunk), :], own[rows(chunk), :])
-            own[rows(chunk), :] = lax.select(flags[3] == 1, down[rows(chunk), :], part)
-
-        store.start()
+
+    @pl.loop(0, chunks + lag * last)
+    def _(step):
+        advance(step - lag * me, up, up_send, up_recv, me == 0, me == last, above, flags[0])
+        advance(step - lag * (last - me), down, down_send, down_recv, me == last, me == 0, below, flags[1])
+        done = step - lag * last
+
+        @pl.when(done >= 0)
+        def _():
+            part = lax.select(flags[2] == 1, up[rows(done), :], own[rows(done), :])
+            own[rows(done), :] = lax.select(flags[3] == 1, down[rows(done), :], part)
+
+        for place, store in enumerate(stores):
+            pl.when(done == (place + 1) * each - 1)(store.start)
+
+    @pl.loop(0, chunks)
+    def _(chunk):
+        @pl.when(me < last)
+        def _():
+            copy(up, up_send, up_recv, chunk, above).wait_send()
+
+        @pl.when(me > 0)
+        def _():
+            copy(down, down_send, down_recv, chunk, below).wait_send()
+
     for store in stores:
         store.wait()
 

time: 305 us -> 302 us (level)
  no operation moved by 1% of the time
where the time goes in v3:
time: 302 us
  Pallas kernels  185 us (61%)
  waiting for transfers between devices  53.9 us (18%)
  other arithmetic  25 us (8%)
  between operations  15.4 us (5%)
  local copies, waits for them, and re-layouts  11.9 us (4%)
  starting transfers between devices  8.68 us (3%)
    pallas_call x1, Pallas kernels, chain(): pl.pallas_call(functools.partial(chain_kernel, size, chunks), out_shape=[...  169 us
    all_gather x1, waiting for transfers between devices, body(): context = lax.all_gather(context, 'fsdp', axis=0)  19.4 us
    all_to_all x1, waiting for transfers between devices, body(): lax.all_to_all(stacked, 'fsdp', split_axis=0, concat_axis=0, tiled=True)  19.2 us
    broadcast_in_dim x3, other arithmetic, body(): return (new_proj[None], new_first[None], new_second[None])  16.8 us
    pallas_call x1, Pallas kernels, member_step(): pl.pallas_call(step_kernel, grid=(rows // tile,), out_shape=[jax.ShapeDty...  16.6 us
    all_to_all x1, waiting for transfers between devices, body(): lax.all_to_all(columns, 'fsdp', split_axis=0, concat_axis=0, tiled=True)  15.3 us
    unnamed x16, local copies, waits for them, and re-layouts  6.9 us
  transfers between devices with their start and end apart: 3, of which 3 were waited for; matrix products, arithmetic and copies ran while one was open for 1% of the time, Pallas kernels for 0%

profile of v3, /device:TPU:0, one launch (start us, length us, event | category | flops | bytes accessed | tf_op | source)
XLA Modules:
  0.0 301.6 jit_solution(8625676271396815958)
XLA Ops:
  7.2 1.5 copy.53
  8.6 1.5 copy.54
  10.1 1.5 copy.55
  11.6 0.2 maximum_bitcast_fusion
  11.7 1.6 copy.56
  13.3 5.2 %all-to-all-start.1 = ((bf16[4,3,128,512]{3,2,1,0:T(8,128)(2,1)}), bf16[4,3,128,512]{3,2,1,0:T(8,128)(2,1)S(1)}, u32[]{:S(2)}, u32[]{:S(2)}) async-start(bf16[4,3,128,512]{3,2,1,0:T(8,128)(2,1)} %copy.56), calls=%async_computation.1 | async-start | bytes 3145728 | tf_op jit(solution)/shard_map/all_to_all | solution.py:217
  18.5 0.0 all-gather.2.cloned.1.call-start
  18.5 0.1 iota_compare_fusion
  18.6 19.2 %all-to-all-done.1 = bf16[4,3,128,512]{3,2,1,0:T(8,128)(2,1)S(1)} async-done(((bf16[4,3,128,512]{3,2,1,0:T(8,128)(2,1)}), bf16[4,3,128,512]{3,2,1,0:T(8,128)(2,1)S(1)}, u32[]{:S(2)}, u32[]{:S(2)}) %all-to-all-start.1) | async-done | bytes 1572896 | tf_op jit(solution)/shard_map/all_to_all | solution.py:217
  37.7 0.1 fusion.29
  37.8 0.1 reshape.42
  38.0 0.1 squeeze.21
  38.1 0.1 squeeze.20
  38.2 0.7 fusion.22
  38.9 2.4 fusion.30
  41.3 0.0 copy-start.3
  41.3 0.5 fusion.18
  41.8 0.0 copy-start.4
  41.9 0.0 copy-start.5
  41.9 1.0 copy.61
  42.9 0.0 all-gather.2.cloned.1.call-update
  42.9 0.0 copy-done.3
  42.9 1.3 copy.51
  44.2 3.5 %all-to-all-start = ((bf16[4,128,1024]{1,2,0:T(8,128)(2,1)}), bf16[4,128,1024]{1,2,0:T(8,128)(2,1)S(1)}, u32[]{:S(2)}, u32[]{:S(2)}) async-start(bf16[4,128,1024]{1,2,0:T(8,128)(2,1)} %bitcast.1), calls=%async_computation | async-start | bytes 2097152 | tf_op jit(solution)/shard_map/all_to_all | solution.py:218
  47.7 0.0 copy-done.4
  47.8 0.0 copy-done.5
  47.8 0.7 compare_and_fusion.2
  48.4 0.1 convert_reduce_fusion
  48.6 0.7 reduce_max.28
  49.3 0.6 reduce_max.29
  51.1 15.3 %all-to-all-done = bf16[4,128,1024]{1,2,0:T(8,128)(2,1)S(1)} async-done(((bf16[4,128,1024]{1,2,0:T(8,128)(2,1)}), bf16[4,128,1024]{1,2,0:T(8,128)(2,1)S(1)}, u32[]{:S(2)}, u32[]{:S(2)}) %all-to-all-start) | async-done | bytes 1048608 | tf_op jit(solution)/shard_map/all_to_all | solution.py:218
  66.4 0.1 bitcast_bitcast_fusion.grad_ref
  66.5 19.4 %all-gather.2.cloned.1.call-done = bf16[4,512,512]{2,1,0:T(8,128)(2,1)} async-done(((bf16[1,512,512]{2,1,0:T(8,128)(2,1)}), bf16[4,512,512]{2,1,0:T(8,128)(2,1)}) %all-gather.2.cloned.1.call-update) | async-done | bytes 2097168 | tf_op jit(solution)/shard_map/all_gather | solution.py:224
  86.0 1.9 copy.66
  87.9 16.6 %shard_map.121 = (bf16[1024,2048]{1,0:T(8,128)(2,1)}, bf16[1024,2048]{1,0:T(8,128)(2,1)}, bf16[1024,2048]{1,0:T(8,128)(2,1)}) custom-call(bf16[1024,512]{1,0:T(8,128)(2,1)S(1)} %bitcast_bitcast_fusion.grad_ref, bf16[512,2048]{1,0:T(8,128)(2,1)S(1)} %bitcast.66, bf16[1024,2048]{1,0:T(8,128)(2,1)} %bitcast.70, f32[1024,2048]{1,0:T(8,128)} %bitcast.67, ...), custom_call_target="tpu_custom_call" | custom-call | tf_op jit(solution)/shard_map/pallas_call | solution.py:157
  104.5 172.3 %while.15 = (s32[]{:T(128)}, bf16[1024,2048]{1,0:T(8,128)(2,1)}, bf16[1024,2048]{1,0:T(8,128)(2,1)}, bf16[1024,2048]{1,0:T(8,128)(2,1)}, s32[]{:T(128)}, /*index...) while((s32[]{:T(128)}, bf16[1024,2048]{1,0:T(8,128)(2,1)}, ...), condition=%wide.region_12.13_spmd.clone, body=%wide.region_7.12_spmd.clone.sunk | while | flops 126 | bytes 261 | solution.py:254
  104.5 0.8 and_reduce_fusion.6
  105.2 2.7 add_convert_fusion.2.flags
  107.9 168.6 %body.1 = (bf16[1024,2048]{1,0:T(8,128)(2,1)}, bf16[1024,2048]{1,0:T(8,128)(2,1)}, bf16[1024,2048]{1,0:T(8,128)(2,1)}) custom-call(s32[4]{0:T(128)S(1)} %add_convert_fusion.2.flags, bf16[1024,2048]{1,0:T(8,128)(2,1)} %get-tuple-element.243.one_in, ...), custom_call_target="tpu_custom_call", output_to_operand_aliasing={{0}: (1, {}), {1}: (2, {}), {2}: (3, {})} | custom-call | tf_op jit(solution)/shard_map/while/body/pallas_call | solution.py:122
  276.7 0.0 copy-start.1
  276.7 6.8 %bitcast_convert_fusion = f32[1,1024,2048]{2,1,0:T(8,128)} fusion(bf16[1024,2048]{1,0:T(8,128)(2,1)} %get-tuple-element.79), kind=kLoop, calls=%fused_computation.13 | loop fusion | flops 2097152 | bytes 12582912 | tf_op jit(solution)/shard_map/broadcast_in_dim | solution.py:263
  283.5 0.0 copy-done.1
  283.5 0.0 copy-start
  283.5 0.0 copy-start.2
  283.5 5.3 %bitcast_convert_fusion.1 = f32[1,1024,2048]{2,1,0:T(8,128)} fusion(bf16[1024,2048]{1,0:T(8,128)(2,1)S(1)} %copy-done.1), kind=kLoop, calls=%fused_computation.14 | loop fusion | flops 2097152 | bytes 12582912 | tf_op jit(solution)/shard_map/broadcast_in_dim | solution.py:263
  288.9 0.0 copy-done
  288.9 1.2 copy-done.2
  290.0 4.7 %fusion.5 = bf16[1,1024,2048]{2,1,0:T(8,128)(2,1)} fusion(bf16[1024,2048]{1,0:T(8,128)(2,1)S(1)} %copy-done, bf16[1,1024,2048]{2,1,0:T(8,128)(2,1)S(1)} %copy-done.2, pred[]{:T(512)} %get-tuple-element.141), kind=kLoop, calls=%fused_computation.12 | loop fusion | flops 10485760 | bytes 12582913 | tf_op jit(solution)/shard_map/broadcast_in_dim | solution.py:263
Async XLA Ops:
  13.3 24.4 %all-to-all-start.1 = ((bf16[4,3,128,512]{3,2,1,0:T(8,128)(2,1)}), bf16[4,3,128,512]{3,2,1,0:T(8,128)(2,1)S(1)}, u32[]{:S(2)}, u32[]{:S(2)}) async-start(bf16[4,3,128,512]{3,2,1,0:T(8,128)(2,1)} %copy.56), calls=%async_computation.1 | async-start | bytes 3145728 | tf_op jit(solution)/shard_map/all_to_all | solution.py:217
  18.5 67.5 %all-gather.2.cloned.1.call-start = ((), (), s32[]{:S(2)}) async-start(), calls=%async_computation.2 | async-start | bytes 2621440 | tf_op jit(solution)/shard_map/all_gather | solution.py:224
  41.3 1.6 copy-start.3
  41.8 5.9 %copy-start.4 = (s32[8]{0:T(128)S(1)}, s32[8]{0:T(128)}, u32[]{:S(2)}) copy-start(s32[8]{0:T(128)} %param.20) | copy-start | bytes 100
  41.9 5.9 %copy-start.5 = (s32[8]{0:T(128)S(1)}, s32[8]{0:T(128)}, u32[]{:S(2)}) copy-start(s32[8]{0:T(128)} %param.21) | copy-start | bytes 100
  44.2 22.2 %all-to-all-start = ((bf16[4,128,1024]{1,2,0:T(8,128)(2,1)}), bf16[4,128,1024]{1,2,0:T(8,128)(2,1)S(1)}, u32[]{:S(2)}, u32[]{:S(2)}) async-start(bf16[4,128,1024]{1,2,0:T(8,128)(2,1)} %bitcast.1), calls=%async_computation | async-start | bytes 2097152 | tf_op jit(solution)/shard_map/all_to_all | solution.py:218
  276.7 6.8 %copy-start.1 = (bf16[1024,2048]{1,0:T(8,128)(2,1)S(1)}, bf16[1024,2048]{1,0:T(8,128)(2,1)}, u32[]{:S(2)}) copy-start(bf16[1024,2048]{1,0:T(8,128)(2,1)} %get-tuple-element.78) | copy-start | bytes 12582916
  283.5 5.3 %copy-start = (bf16[1024,2048]{1,0:T(8,128)(2,1)S(1)}, bf16[1024,2048]{1,0:T(8,128)(2,1)}, u32[]{:S(2)}) copy-start(bf16[1024,2048]{1,0:T(8,128)(2,1)} %get-tuple-element.77) | copy-start | bytes 12582916
  283.5 6.5 %copy-start.2 = (bf16[1,1024,2048]{2,1,0:T(8,128)(2,1)S(1)}, bf16[1,1024,2048]{2,1,0:T(8,128)(2,1)}, u32[]{:S(2)}) copy-start(bf16[1,1024,2048]{2,1,0:T(8,128)(2,1)} %param.19) | copy-start | bytes 12582916
Sparse Core Ops, SparseCore 0:
  43.0 42.8 all-gather.1
